TPU v7x, 256 devices: a whole 4x4x8 slice. The times are simulated.
256 devices in a mesh: tile: 64 (over x, z_hi, y, core), vis: 4 (over z_lo).
Axes of the slice: x: 4, y: 4, z: 8 (z_hi: 2, z_lo: 4; z = z_hi * 4 + z_lo), core: 2. Of those that a mesh axis runs over, the one named last changes fastest.
Arguments:
- model_image: float32 [512, 32768], P(('tile', 'vis')), may hold values from -1.2 to 1.2
- psf: float32 [512, 512], P(('tile', 'vis')), may hold values from -1 to 2
- kernel_table: float32 [128, 8], replicated, may hold values from 0.1 to 1
- observed: float32 [2, 4, 1024, 256], P(None, 'vis', 'tile'), may hold values from -3.6 to 3.6
- visit_tile: int32 [4, 1024], P('vis', 'tile'), may hold values from 0 to 15, as said below
- visit_count: int32 [4, 1024], P('vis', 'tile'), may hold values from 1 to 256, as said below
- cell_offset: int32 [2, 4, 1024, 256], P(None, 'vis', 'tile'), may hold values from 0 to 120
- kernel_row: int32 [2, 4, 1024, 256], P(None, 'vis', 'tile'), may hold values from 0 to 127
Outputs:
- model_next: float32 [512, 32768], P(('tile', 'vis'))
- residual_image: float32 [512, 32768], P(('tile', 'vis'))
Inputs may be any that keep to these rules, and one draw needn't show every extreme that they name: `visit_tile`: within the 16 visits of one tile index (positions along the second dimension in blocks of 16), visit j lies in one of the 4 tiles numbered from k * 4 on, k = j // 4. `visit_count`: slots below the count hold visibilities; the others are dead.
All inputs are finite; a program needn't handle non-finite values.
Results may differ from a plain program's by a relative error of at most 0.0051.
Values may be sent and summed in bfloat16 or wider, within the bound.
No kernel may reach another device: no remote copies, remote signals or barrier semaphores. Data moves between devices by JAX's collectives and lax.ppermute only.
A program may use at most 64 MiB of HBM per device.

v0:
```python
import math

import jax
import jax.numpy as jnp
from jax import lax
from jax.sharding import PartitionSpec as P

GU = 32768
GV = 512
UVT = 128
CAP = 256
ITERS = 3


STEP_SIZE = 0.5
THRESHOLD = 0.05
HIGHEST = lax.Precision.HIGHEST


def phase_table(left, right, length, sign):
    turns = left[:, None] * right[None, :] % length
    angle = 2.0 * math.pi / length * turns.astype(jnp.float32)
    return (jnp.cos(angle), sign * jnp.sin(angle))


def contract(form, operand, table):
    return jnp.einsum(form, operand, table, precision=HIGHEST, preferred_element_type=jnp.float32)


def product(form, real_part, imag_part, cosine, sine):
    first = contract(form, real_part, cosine)
    second = contract(form, real_part, sine)
    if imag_part is None:
        return (first, second)
    return (first - contract(form, imag_part, sine), second + contract(form, imag_part, cosine))


def rotate(real_part, imag_part, cosine, sine):
    return (real_part * cosine - imag_part * sine, real_part * sine + imag_part * cosine)


def to_grid(real_part, scale):
    tile_count = lax.axis_size("tile")
    vis_count = lax.axis_size("vis")
    blocks = tile_count * vis_count
    col_width = GU // blocks
    row_count = real_part.shape[0]
    shaped_real = real_part.reshape(row_count, blocks, col_width)
    shaped_imag = None
    cosine, sine = phase_table(jnp.arange(blocks), jnp.arange(blocks), blocks, -1.0)
    first_real, first_imag = product("ram,ap->rpm", shaped_real, shaped_imag, cosine, sine)
    cosine, sine = phase_table(jnp.arange(blocks), jnp.arange(col_width), GU, -1.0)
    first_real, first_imag = rotate(first_real, first_imag, cosine[None], sine[None])
    cosine, sine = phase_table(jnp.arange(col_width), jnp.arange(col_width), col_width, -1.0)
    second_real, second_imag = product("rpm,mq->rqp", first_real, first_imag, cosine, sine)
    moved_real, moved_imag = (
        lax.all_to_all(
            lax.all_to_all(
                second_real.reshape(row_count, GU), "tile", split_axis=1, concat_axis=0, tiled=True
            ),
            "vis",
            split_axis=1,
            concat_axis=0,
            tiled=True,
        ),
        lax.all_to_all(
            lax.all_to_all(
                second_imag.reshape(row_count, GU), "tile", split_axis=1, concat_axis=0, tiled=True
            ),
            "vis",
            split_axis=1,
            concat_axis=0,
            tiled=True,
        ),
    )
    position = jnp.arange(GV)
    source_vis = position // (tile_count * row_count)
    source_tile = position // row_count % tile_count
    image_row = (source_tile * vis_count + source_vis) * row_count + position % row_count
    cosine, sine = phase_table(jnp.arange(GV), image_row, GV, -1.0)
    grid_real, grid_imag = product("pc,kp->kc", moved_real, moved_imag, cosine, sine)
    return (grid_real * scale, grid_imag * scale)


def to_image(real_part, imag_part):
    tile_count = lax.axis_size("tile")
    vis_count = lax.axis_size("vis")
    blocks = tile_count * vis_count
    col_width = real_part.shape[1]
    cosine, sine = phase_table(jnp.arange(GV), jnp.arange(GV), GV, 1.0)
    line_real, line_imag = product("kc,kv->vc", real_part, imag_part, cosine, sine)
    moved_real, moved_imag = (
        lax.all_to_all(
            lax.all_to_all(line_real, "tile", split_axis=0, concat_axis=1, tiled=True),
            "vis",
            split_axis=0,
            concat_axis=1,
            tiled=True,
        ),
        lax.all_to_all(
            lax.all_to_all(line_imag, "tile", split_axis=0, concat_axis=1, tiled=True),
            "vis",
            split_axis=0,
            concat_axis=1,
            tiled=True,
        ),
    )
    row_count = moved_real.shape[0]
    position = jnp.arange(blocks)
    block_index = position % tile_count * vis_count + position // tile_count
    cosine, sine = phase_table(block_index, jnp.arange(blocks), blocks, 1.0)
    first_real, first_imag = product(
        "ram,ap->rpm",
        moved_real.reshape(row_count, blocks, col_width),
        moved_imag.reshape(row_count, blocks, col_width),
        cosine,
        sine,
    )
    cosine, sine = phase_table(jnp.arange(blocks), jnp.arange(col_width), GU, 1.0)
    first_real, first_imag = rotate(first_real, first_imag, cosine[None], sine[None])
    cosine, sine = phase_table(jnp.arange(col_width), jnp.arange(col_width), col_width, 1.0)
    image = contract("rpm,mq->rqp", first_real, cosine) - contract("rpm,mq->rqp", first_imag, sine)
    return image.reshape(row_count, GU) / math.sqrt(GV * GU)


def to_tiles(real_part, imag_part):
    tile_rows = GV // UVT
    tile_cols = real_part.shape[1] // UVT

    def arrange(part):
        return (
            part.reshape(tile_rows, UVT, tile_cols, UVT)
            .transpose(2, 0, 1, 3)
            .reshape(tile_cols * tile_rows, UVT, UVT)
        )

    return jnp.concatenate([arrange(real_part), arrange(imag_part)], axis=-1)


def from_tiles(bank, width):
    tile_rows = GV // UVT
    tile_cols = width // UVT

    def restore(part):
        return part.reshape(tile_cols, tile_rows, UVT, UVT).transpose(1, 2, 0, 3).reshape(GV, width)

    return (restore(bank[..., :UVT]), restore(bank[..., UVT:]))


def lookup_taps(table, rows):
    choose = (rows[:, :, None] == jnp.arange(table.shape[0])[None, None, :]).astype(jnp.bfloat16)
    return jnp.einsum("vsr,rk->kvs", choose, table, preferred_element_type=jnp.float32)


def spread_taps(taps, offsets):
    within = jnp.arange(UVT)[None, None, :] - offsets[:, :, None]
    weights = jnp.zeros(offsets.shape + (UVT,), jnp.float32)
    for shift in range(taps.shape[0]):
        weights = weights + jnp.where(within == shift, taps[shift][:, :, None], 0.0)
    return weights


def grid_work(tile_bank, tile_ids, off_row, off_col, taps_row, taps_col, values):
    weight_row = spread_taps(taps_row, off_row).astype(jnp.bfloat16)
    weight_col = spread_taps(taps_col, off_col)
    chosen = jnp.take(tile_bank, tile_ids, axis=0)
    partial_value = jnp.einsum(
        "vsr,vrc->vsc", weight_row, chosen, preferred_element_type=jnp.float32
    )
    model_real = jnp.sum(partial_value[..., :UVT] * weight_col, axis=-1)
    model_imag = jnp.sum(partial_value[..., UVT:] * weight_col, axis=-1)
    resid_real = values[0] - model_real
    resid_imag = values[1] - model_imag
    spread = jnp.concatenate(
        [resid_real[..., None] * weight_col, resid_imag[..., None] * weight_col], axis=-1
    ).astype(jnp.bfloat16)
    contrib = jnp.einsum("vsr,vsc->vrc", weight_row, spread, preferred_element_type=jnp.float32)
    owners = (tile_ids[:, None] == jnp.arange(tile_bank.shape[0])[None, :]).astype(jnp.float32)
    return jnp.einsum(
        "vt,vrc->trc", owners, contrib, precision=HIGHEST, preferred_element_type=jnp.float32
    )


def shards(
    model_image, psf, kernel_table, observed, visit_tile, visit_count, cell_offset, kernel_row
):
    tile_count = lax.axis_size("tile")
    vis_count = lax.axis_size("vis")
    col_width = GU // (tile_count * vis_count)
    unit_scale = 1.0 / math.sqrt(GV * GU)
    grid_real, grid_imag = to_grid(model_image, unit_scale)
    grid_real = grid_real.astype(jnp.bfloat16)
    grid_imag = grid_imag.astype(jnp.bfloat16)
    table = kernel_table.astype(jnp.bfloat16)
    tile_ids = visit_tile[0]
    counts = visit_count[0]
    live = jnp.arange(CAP)[None, :] < counts[:, None]
    values = observed[:, 0]
    taps_row = lookup_taps(table, kernel_row[0, 0]) * live[None].astype(jnp.float32)
    taps_col = lookup_taps(table, kernel_row[1, 0])
    region = (
        lax.all_gather(grid_real, "vis", axis=1, tiled=True),
        lax.all_gather(grid_imag, "vis", axis=1, tiled=True),
    )
    bank = to_tiles(region[0], region[1])
    partial_value = grid_work(
        bank, tile_ids, cell_offset[0, 0], cell_offset[1, 0], taps_row, taps_col, values
    )
    part_real, part_imag = from_tiles(partial_value, col_width * vis_count)
    res_real, res_imag = (
        lax.psum_scatter(part_real, "vis", scatter_dimension=1, tiled=True),
        lax.psum_scatter(part_imag, "vis", scatter_dimension=1, tiled=True),
    )
    residual_image = to_image(res_real, res_imag)
    row_count = psf.shape[0]
    padded = jnp.concatenate(
        [psf[:, GV // 2 :], jnp.zeros((row_count, GU - GV), jnp.float32), psf[:, : GV // 2]], axis=1
    )
    psf_real, psf_imag = to_grid(padded, 1.0)
    model_now = model_image
    for step in range(ITERS):
        if step == 0:
            gradient = residual_image
        else:
            change_real, change_imag = to_grid(model_now - model_image, unit_scale)
            blur_real, blur_imag = rotate(change_real, change_imag, psf_real, psf_imag)
            gradient = residual_image - to_image(blur_real, blur_imag)
        moved = model_now + STEP_SIZE * gradient
        model_now = moved - jnp.clip(moved, -THRESHOLD, THRESHOLD)
    return (model_now, residual_image)


def solution(mesh):
    placed = (
        P(("tile", "vis"), None),
        P(("tile", "vis"), None),
        P(),
        P(None, "vis", "tile", None),
        P("vis", "tile"),
        P("vis", "tile"),
        P(None, "vis", "tile", None),
        P(None, "vis", "tile", None),
    )
    return jax.shard_map(
        shards,
        mesh=mesh,
        in_specs=placed,
        out_specs=(P(("tile", "vis"), None), P(("tile", "vis"), None)),
        check_vma=False,
    )
```

profile of v0, /device:TPU:1, one launch (start us, length us, event | category | flops | bytes accessed | tf_op | source)
XLA Modules:
  0.0 668.7 jit_solution(2823633328467907200)
XLA Ops:
  14.8 15.6 %all-to-all-start = ((f32[2,64,512]{2,0,1:T(2,128)}), f32[2,64,512]{2,0,1:T(2,128)S(1)}, u32[]{:S(2)}, u32[]{:S(2)}) async-start(f32[2,64,512]{2,0,1:T(2,128)} %copy.45), calls=%async_computation | async-start | bytes 524288 | tf_op jit(solution)/shard_map/all_to_all | solution.py:58
  36.6 7.6 %all-to-all-done = f32[2,64,512]{2,0,1:T(2,128)S(1)} async-done(((f32[2,64,512]{2,0,1:T(2,128)}), f32[2,64,512]{2,0,1:T(2,128)S(1)}, u32[]{:S(2)}, u32[]{:S(2)}) %all-to-all-start) | async-done | bytes 262176 | tf_op jit(solution)/shard_map/all_to_all | solution.py:58
  50.4 12.8 %all-to-all-done.2 = f32[2,64,512]{2,0,1:T(2,128)S(1)} async-done(((f32[2,64,512]{2,0,1:T(2,128)}), f32[2,64,512]{2,0,1:T(2,128)S(1)}, u32[]{:S(2)}, u32[]{:S(2)}) %all-to-all-start.2) | async-done | bytes 262176 | tf_op jit(solution)/shard_map/all_to_all | solution.py:67
  70.4 6.5 all-to-all-done.1
  96.6 13.0 %all_gather.6 = bf16[512,512]{1,0:T(8,128)(2,1)S(1)} all-gather(bf16[512,128]{1,0:T(8,128)(2,1)S(1)} %fusion.50), channel_id=1, replica_groups=mesh['tile'=64,'vis'=4] {'vis'}, dimensions={1}, use_global_device_ids=true | all-gather | bytes 655360 | tf_op jit(solution)/shard_map/all_gather | solution.py:202
  115.5 12.5 %all_gather.7 = bf16[512,512]{1,0:T(8,128)(2,1)S(1)} all-gather(bf16[512,128]{1,0:T(8,128)(2,1)S(1)} %fusion.51), channel_id=1, replica_groups=mesh['tile'=64,'vis'=4] {'vis'}, dimensions={1}, use_global_device_ids=true | all-gather | bytes 655360 | tf_op jit(solution)/shard_map/all_gather | solution.py:203
  149.1 10.1 %all-to-all-start.12 = ((f32[2,64,512]{2,0,1:T(2,128)}), f32[2,64,512]{2,0,1:T(2,128)S(1)}, u32[]{:S(2)}, u32[]{:S(2)}) async-start(f32[2,64,512]{2,0,1:T(2,128)} %copy.65), calls=%async_computation.14 | async-start | bytes 524288 | tf_op jit(solution)/shard_map/all_to_all | solution.py:58
  161.6 15.8 %all-to-all-done.12 = f32[2,64,512]{2,0,1:T(2,128)S(1)} async-done(((f32[2,64,512]{2,0,1:T(2,128)}), f32[2,64,512]{2,0,1:T(2,128)S(1)}, u32[]{:S(2)}, u32[]{:S(2)}) %all-to-all-start.12) | async-done | bytes 262176 | tf_op jit(solution)/shard_map/all_to_all | solution.py:58
  188.9 24.0 %reduce-scatter.5.cloned.1.call-done = f32[512,128]{1,0:T(8,128)} async-done(((f32[512,512]{1,0:T(8,128)}), f32[512,128]{1,0:T(8,128)}) %reduce-scatter.5.cloned.1.call-update) | async-done | bytes 262160 | tf_op jit(solution)/shard_map/reduce_scatter | solution.py:212
  213.0 7.7 %fusion.47 = f32[64,8,128]{2,1,0:T(8,128)} fusion(f32[512,128]{1,0:T(8,128)S(1)} %fusion.82, f32[512,128]{1,0:T(8,128)} %reduce-scatter.5.cloned.1.call-done), kind=kOutput, calls=%fused_computation.93 | convolution fusion | flops 406388736 | bytes 786432 | tf_op jit(solution)/shard_map/kc,kv->vc/dot_general | solution.py:27
  220.7 10.4 %all-to-all-start.4 = ((f32[64,8,128]{2,1,0:T(8,128)}), f32[64,8,128]{2,1,0:T(8,128)S(1)}, u32[]{:S(2)}, u32[]{:S(2)}) async-start(f32[64,8,128]{2,1,0:T(8,128)} %fusion.47), calls=%async_computation.6 | async-start | bytes 524288 | tf_op jit(solution)/shard_map/all_to_all | solution.py:94
  237.2 6.7 %fusion.46 = f32[64,8,128]{2,1,0:T(8,128)} fusion(f32[512,128]{1,0:T(8,128)S(1)} %fusion.90, f32[512,128]{1,0:T(8,128)S(1)} %copy-done.9), kind=kOutput, calls=%fused_computation.91 | convolution fusion | flops 406388736 | bytes 786432 | tf_op jit(solution)/shard_map/kc,kv->vc/dot_general | solution.py:27
  244.8 11.9 %all-to-all-start.6 = ((f32[64,8,128]{2,1,0:T(8,128)}), f32[64,8,128]{2,1,0:T(8,128)S(1)}, u32[]{:S(2)}, u32[]{:S(2)}) async-start(f32[64,8,128]{2,1,0:T(8,128)} %fusion.46), calls=%async_computation.8 | async-start | bytes 524288 | tf_op jit(solution)/shard_map/all_to_all | solution.py:101
  257.6 12.9 %all-to-all-done.6 = f32[64,8,128]{2,1,0:T(8,128)S(1)} async-done(((f32[64,8,128]{2,1,0:T(8,128)}), f32[64,8,128]{2,1,0:T(8,128)S(1)}, u32[]{:S(2)}, u32[]{:S(2)}) %all-to-all-start.6) | async-done | bytes 262176 | tf_op jit(solution)/shard_map/all_to_all | solution.py:101
  315.9 9.6 %all-to-all-start.8 = ((f32[2,64,512]{2,0,1:T(2,128)}), f32[2,64,512]{2,0,1:T(2,128)S(1)}, u32[]{:S(2)}, u32[]{:S(2)}) async-start(f32[2,64,512]{2,0,1:T(2,128)} %copy.61), calls=%async_computation.10 | async-start | bytes 524288 | tf_op jit(solution)/shard_map/all_to_all | solution.py:58
  327.9 11.7 %all-to-all-done.8 = f32[2,64,512]{2,0,1:T(2,128)S(1)} async-done(((f32[2,64,512]{2,0,1:T(2,128)}), f32[2,64,512]{2,0,1:T(2,128)S(1)}, u32[]{:S(2)}, u32[]{:S(2)}) %all-to-all-start.8) | async-done | bytes 262176 | tf_op jit(solution)/shard_map/all_to_all | solution.py:58
  339.5 6.5 all-to-all-start.10
  405.6 6.8 %fusion.43 = f32[64,8,128]{2,1,0:T(8,128)} fusion(f32[512,128]{1,0:T(8,128)S(1)} %fusion.79, f32[512,128]{1,0:T(8,128)S(1)} %get-tuple-element.8), kind=kOutput, calls=%fused_computation.83 | convolution fusion | flops 406388736 | bytes 786432 | tf_op jit(solution)/shard_map/kc,kv->vc/dot_general | solution.py:27
  412.3 8.8 %all-to-all-start.16 = ((f32[64,8,128]{2,1,0:T(8,128)}), f32[64,8,128]{2,1,0:T(8,128)S(1)}, u32[]{:S(2)}, u32[]{:S(2)}) async-start(f32[64,8,128]{2,1,0:T(8,128)} %fusion.43), calls=%async_computation.18 | async-start | bytes 524288 | tf_op jit(solution)/shard_map/all_to_all | solution.py:94
  427.3 6.7 %fusion.42 = f32[64,8,128]{2,1,0:T(8,128)} fusion(f32[512,128]{1,0:T(8,128)S(1)} %fusion.87, f32[512,128]{1,0:T(8,128)S(1)} %get-tuple-element.8), kind=kOutput, calls=%fused_computation.81 | convolution fusion | flops 406388736 | bytes 786432 | tf_op jit(solution)/shard_map/kc,kv->vc/dot_general | solution.py:27
  435.0 11.8 %all-to-all-start.18 = ((f32[64,8,128]{2,1,0:T(8,128)}), f32[64,8,128]{2,1,0:T(8,128)S(1)}, u32[]{:S(2)}, u32[]{:S(2)}) async-start(f32[64,8,128]{2,1,0:T(8,128)} %fusion.42), calls=%async_computation.20 | async-start | bytes 524288 | tf_op jit(solution)/shard_map/all_to_all | solution.py:101
  447.7 12.9 %all-to-all-done.18 = f32[64,8,128]{2,1,0:T(8,128)S(1)} async-done(((f32[64,8,128]{2,1,0:T(8,128)}), f32[64,8,128]{2,1,0:T(8,128)S(1)}, u32[]{:S(2)}, u32[]{:S(2)}) %all-to-all-start.18) | async-done | bytes 262176 | tf_op jit(solution)/shard_map/all_to_all | solution.py:101
  494.4 8.3 %all-to-all-start.20 = ((f32[2,64,512]{2,0,1:T(2,128)}), f32[2,64,512]{2,0,1:T(2,128)S(1)}, u32[]{:S(2)}, u32[]{:S(2)}) async-start(f32[2,64,512]{2,0,1:T(2,128)} %copy.73), calls=%async_computation.22 | async-start | bytes 524288 | tf_op jit(solution)/shard_map/all_to_all | solution.py:58
  505.1 11.6 %all-to-all-done.20 = f32[2,64,512]{2,0,1:T(2,128)S(1)} async-done(((f32[2,64,512]{2,0,1:T(2,128)}), f32[2,64,512]{2,0,1:T(2,128)S(1)}, u32[]{:S(2)}, u32[]{:S(2)}) %all-to-all-start.20) | async-done | bytes 262176 | tf_op jit(solution)/shard_map/all_to_all | solution.py:58
  516.7 6.9 %all-to-all-start.22 = ((f32[2,64,512]{2,0,1:T(2,128)}), f32[2,64,512]{2,0,1:T(2,128)S(1)}, u32[]{:S(2)}, u32[]{:S(2)}) async-start(f32[2,64,512]{2,0,1:T(2,128)} %copy.75), calls=%async_computation.24 | async-start | bytes 524288 | tf_op jit(solution)/shard_map/all_to_all | solution.py:67
  524.5 12.9 %all-to-all-done.22 = f32[2,64,512]{2,0,1:T(2,128)S(1)} async-done(((f32[2,64,512]{2,0,1:T(2,128)}), f32[2,64,512]{2,0,1:T(2,128)S(1)}, u32[]{:S(2)}, u32[]{:S(2)}) %all-to-all-start.22) | async-done | bytes 262176 | tf_op jit(solution)/shard_map/all_to_all | solution.py:67
  577.9 6.8 %fusion.39 = f32[64,8,128]{2,1,0:T(8,128)} fusion(f32[512,128]{1,0:T(8,128)S(1)} %fusion.76, f32[512,128]{1,0:T(8,128)S(1)} %get-tuple-element.6), kind=kOutput, calls=%fused_computation.75 | convolution fusion | flops 406388736 | bytes 786432 | tf_op jit(solution)/shard_map/kc,kv->vc/dot_general | solution.py:27
  584.7 8.2 %all-to-all-start.24 = ((f32[64,8,128]{2,1,0:T(8,128)}), f32[64,8,128]{2,1,0:T(8,128)S(1)}, u32[]{:S(2)}, u32[]{:S(2)}) async-start(f32[64,8,128]{2,1,0:T(8,128)} %fusion.39), calls=%async_computation.26 | async-start | bytes 524288 | tf_op jit(solution)/shard_map/all_to_all | solution.py:94
  599.0 6.7 %fusion.38 = f32[64,8,128]{2,1,0:T(8,128)} fusion(f32[512,128]{1,0:T(8,128)S(1)} %fusion.84, f32[512,128]{1,0:T(8,128)S(1)} %get-tuple-element.6), kind=kOutput, calls=%fused_computation.73 | convolution fusion | flops 406388736 | bytes 786432 | tf_op jit(solution)/shard_map/kc,kv->vc/dot_general | solution.py:27
  606.7 11.8 %all-to-all-start.26 = ((f32[64,8,128]{2,1,0:T(8,128)}), f32[64,8,128]{2,1,0:T(8,128)S(1)}, u32[]{:S(2)}, u32[]{:S(2)}) async-start(f32[64,8,128]{2,1,0:T(8,128)} %fusion.38), calls=%async_computation.28 | async-start | bytes 524288 | tf_op jit(solution)/shard_map/all_to_all | solution.py:101
  619.4 12.9 %all-to-all-done.26 = f32[64,8,128]{2,1,0:T(8,128)S(1)} async-done(((f32[64,8,128]{2,1,0:T(8,128)}), f32[64,8,128]{2,1,0:T(8,128)S(1)}, u32[]{:S(2)}, u32[]{:S(2)}) %all-to-all-start.26) | async-done | bytes 262176 | tf_op jit(solution)/shard_map/all_to_all | solution.py:101
  639.4 6.6 all-to-all-done.25
  (230 shorter events, 318.4 us)
Async XLA Ops:
  14.8 29.4 %all-to-all-start = ((f32[2,64,512]{2,0,1:T(2,128)}), f32[2,64,512]{2,0,1:T(2,128)S(1)}, u32[]{:S(2)}, u32[]{:S(2)}) async-start(f32[2,64,512]{2,0,1:T(2,128)} %copy.45), calls=%async_computation | async-start | bytes 524288 | tf_op jit(solution)/shard_map/all_to_all | solution.py:58
  44.2 19.0 %all-to-all-start.2 = ((f32[2,64,512]{2,0,1:T(2,128)}), f32[2,64,512]{2,0,1:T(2,128)S(1)}, u32[]{:S(2)}, u32[]{:S(2)}) async-start(f32[2,64,512]{2,0,1:T(2,128)} %copy.47), calls=%async_computation.2 | async-start | bytes 524288 | tf_op jit(solution)/shard_map/all_to_all | solution.py:67
  63.2 13.7 %all-to-all-start.1 = ((f32[128,4,128]{2,0,1:T(8,128)}), f32[128,4,128]{2,0,1:T(8,128)S(1)}, u32[]{:S(2)}, u32[]{:S(2)}) async-start(f32[128,4,128]{2,0,1:T(8,128)} %copy.46), calls=%async_computation.1 | async-start | bytes 524288 | tf_op jit(solution)/shard_map/all_to_all | solution.py:57
  76.8 14.2 %all-to-all-start.3 = ((f32[128,4,128]{2,0,1:T(8,128)}), f32[128,4,128]{2,0,1:T(8,128)S(1)}, u32[]{:S(2)}, u32[]{:S(2)}) async-start(f32[128,4,128]{2,0,1:T(8,128)} %copy.48), calls=%async_computation.3 | async-start | bytes 524288 | tf_op jit(solution)/shard_map/all_to_all | solution.py:66
  81.0 101.5 %reduce-scatter.3.cloned.1.call-start = ((), (), s32[]{:S(2)}) async-start(), calls=%async_computation.30 | async-start | bytes 1310720 | tf_op jit(solution)/shard_map/reduce_scatter | solution.py:211
  142.2 70.8 %reduce-scatter.5.cloned.1.call-start = ((), (), s32[]{:S(2)}) async-start(), calls=%async_computation.31 | async-start | bytes 1310720 | tf_op jit(solution)/shard_map/reduce_scatter | solution.py:212
  149.1 28.3 %all-to-all-start.12 = ((f32[2,64,512]{2,0,1:T(2,128)}), f32[2,64,512]{2,0,1:T(2,128)S(1)}, u32[]{:S(2)}, u32[]{:S(2)}) async-start(f32[2,64,512]{2,0,1:T(2,128)} %copy.65), calls=%async_computation.14 | async-start | bytes 524288 | tf_op jit(solution)/shard_map/all_to_all | solution.py:58
  177.4 43.2 %all-to-all-start.14 = ((f32[2,64,512]{2,0,1:T(2,128)}), f32[2,64,512]{2,0,1:T(2,128)S(1)}, u32[]{:S(2)}, u32[]{:S(2)}) async-start(f32[2,64,512]{2,0,1:T(2,128)} %copy.67), calls=%async_computation.16 | async-start | bytes 524288 | tf_op jit(solution)/shard_map/all_to_all | solution.py:67
  188.9 42.1 %copy-start.8 = (f32[512,128]{1,0:T(8,128)S(1)}, f32[512,128]{1,0:T(8,128)}, u32[]{:S(2)}) copy-start(f32[512,128]{1,0:T(8,128)} %reduce-scatter.3.cloned.1.call-done) | copy-start | bytes 786436
  220.7 24.1 %all-to-all-start.4 = ((f32[64,8,128]{2,1,0:T(8,128)}), f32[64,8,128]{2,1,0:T(8,128)S(1)}, u32[]{:S(2)}, u32[]{:S(2)}) async-start(f32[64,8,128]{2,1,0:T(8,128)} %fusion.47), calls=%async_computation.6 | async-start | bytes 524288 | tf_op jit(solution)/shard_map/all_to_all | solution.py:94
  244.8 25.7 %all-to-all-start.6 = ((f32[64,8,128]{2,1,0:T(8,128)}), f32[64,8,128]{2,1,0:T(8,128)S(1)}, u32[]{:S(2)}, u32[]{:S(2)}) async-start(f32[64,8,128]{2,1,0:T(8,128)} %fusion.46), calls=%async_computation.8 | async-start | bytes 524288 | tf_op jit(solution)/shard_map/all_to_all | solution.py:101
  270.5 12.0 %all-to-all-start.5 = ((f32[4,2,8192]{2,1,0:T(2,128)}), f32[4,2,8192]{2,1,0:T(2,128)S(1)}, u32[]{:S(2)}, u32[]{:S(2)}) async-start(f32[4,2,8192]{2,1,0:T(2,128)} %all_to_all.369), calls=%async_computation.7 | async-start | bytes 524288 | tf_op jit(solution)/shard_map/all_to_all | solution.py:93
  282.5 12.1 %all-to-all-start.7 = ((f32[4,2,8192]{2,1,0:T(2,128)}), f32[4,2,8192]{2,1,0:T(2,128)S(1)}, u32[]{:S(2)}, u32[]{:S(2)}) async-start(f32[4,2,8192]{2,1,0:T(2,128)} %all_to_all.375), calls=%async_computation.9 | async-start | bytes 524288 | tf_op jit(solution)/shard_map/all_to_all | solution.py:100
  294.6 11.1 %all-to-all-start.13 = ((f32[128,4,128]{2,0,1:T(8,128)}), f32[128,4,128]{2,0,1:T(8,128)S(1)}, u32[]{:S(2)}, u32[]{:S(2)}) async-start(f32[128,4,128]{2,0,1:T(8,128)} %copy.66), calls=%async_computation.15 | async-start | bytes 524288 | tf_op jit(solution)/shard_map/all_to_all | solution.py:57
  305.7 10.1 %all-to-all-start.15 = ((f32[128,4,128]{2,0,1:T(8,128)}), f32[128,4,128]{2,0,1:T(8,128)S(1)}, u32[]{:S(2)}, u32[]{:S(2)}) async-start(f32[128,4,128]{2,0,1:T(8,128)} %copy.68), calls=%async_computation.17 | async-start | bytes 524288 | tf_op jit(solution)/shard_map/all_to_all | solution.py:66
  315.9 23.7 %all-to-all-start.8 = ((f32[2,64,512]{2,0,1:T(2,128)}), f32[2,64,512]{2,0,1:T(2,128)S(1)}, u32[]{:S(2)}, u32[]{:S(2)}) async-start(f32[2,64,512]{2,0,1:T(2,128)} %copy.61), calls=%async_computation.10 | async-start | bytes 524288 | tf_op jit(solution)/shard_map/all_to_all | solution.py:58
  339.5 20.3 %all-to-all-start.10 = ((f32[2,64,512]{2,0,1:T(2,128)}), f32[2,64,512]{2,0,1:T(2,128)S(1)}, u32[]{:S(2)}, u32[]{:S(2)}) async-start(f32[2,64,512]{2,0,1:T(2,128)} %copy.63), calls=%async_computation.12 | async-start | bytes 524288 | tf_op jit(solution)/shard_map/all_to_all | solution.py:67
  359.8 15.4 %all-to-all-start.9 = ((f32[128,4,128]{2,0,1:T(8,128)}), f32[128,4,128]{2,0,1:T(8,128)S(1)}, u32[]{:S(2)}, u32[]{:S(2)}) async-start(f32[128,4,128]{2,0,1:T(8,128)} %copy.62), calls=%async_computation.11 | async-start | bytes 524288 | tf_op jit(solution)/shard_map/all_to_all | solution.py:57
  375.2 14.5 %all-to-all-start.11 = ((f32[128,4,128]{2,0,1:T(8,128)}), f32[128,4,128]{2,0,1:T(8,128)S(1)}, u32[]{:S(2)}, u32[]{:S(2)}) async-start(f32[128,4,128]{2,0,1:T(8,128)} %copy.64), calls=%async_computation.13 | async-start | bytes 524288 | tf_op jit(solution)/shard_map/all_to_all | solution.py:66
  412.3 22.6 %all-to-all-start.16 = ((f32[64,8,128]{2,1,0:T(8,128)}), f32[64,8,128]{2,1,0:T(8,128)S(1)}, u32[]{:S(2)}, u32[]{:S(2)}) async-start(f32[64,8,128]{2,1,0:T(8,128)} %fusion.43), calls=%async_computation.18 | async-start | bytes 524288 | tf_op jit(solution)/shard_map/all_to_all | solution.py:94
  435.0 25.6 %all-to-all-start.18 = ((f32[64,8,128]{2,1,0:T(8,128)}), f32[64,8,128]{2,1,0:T(8,128)S(1)}, u32[]{:S(2)}, u32[]{:S(2)}) async-start(f32[64,8,128]{2,1,0:T(8,128)} %fusion.42), calls=%async_computation.20 | async-start | bytes 524288 | tf_op jit(solution)/shard_map/all_to_all | solution.py:101
  460.6 13.7 %all-to-all-start.17 = ((f32[4,2,8192]{2,1,0:T(2,128)}), f32[4,2,8192]{2,1,0:T(2,128)S(1)}, u32[]{:S(2)}, u32[]{:S(2)}) async-start(f32[4,2,8192]{2,1,0:T(2,128)} %all_to_all.409), calls=%async_computation.19 | async-start | bytes 524288 | tf_op jit(solution)/shard_map/all_to_all | solution.py:93
  467.0 193.5 %copy-start.1 = (f32[1,2,128,256]{3,1,2,0:T(2,128)}, f32[1,2,128,256]{3,1,2,0:T(2,128)S(1)}, u32[]{:S(2)}) copy-start(f32[1,2,128,256]{3,1,2,0:T(2,128)S(1)} %copy.104) | copy-start | bytes 786436
  474.3 9.8 %all-to-all-start.19 = ((f32[4,2,8192]{2,1,0:T(2,128)}), f32[4,2,8192]{2,1,0:T(2,128)S(1)}, u32[]{:S(2)}, u32[]{:S(2)}) async-start(f32[4,2,8192]{2,1,0:T(2,128)} %all_to_all.415), calls=%async_computation.21 | async-start | bytes 524288 | tf_op jit(solution)/shard_map/all_to_all | solution.py:100
  494.4 22.3 %all-to-all-start.20 = ((f32[2,64,512]{2,0,1:T(2,128)}), f32[2,64,512]{2,0,1:T(2,128)S(1)}, u32[]{:S(2)}, u32[]{:S(2)}) async-start(f32[2,64,512]{2,0,1:T(2,128)} %copy.73), calls=%async_computation.22 | async-start | bytes 524288 | tf_op jit(solution)/shard_map/all_to_all | solution.py:58
  516.7 20.7 %all-to-all-start.22 = ((f32[2,64,512]{2,0,1:T(2,128)}), f32[2,64,512]{2,0,1:T(2,128)S(1)}, u32[]{:S(2)}, u32[]{:S(2)}) async-start(f32[2,64,512]{2,0,1:T(2,128)} %copy.75), calls=%async_computation.24 | async-start | bytes 524288 | tf_op jit(solution)/shard_map/all_to_all | solution.py:67
  537.4 10.7 %all-to-all-start.21 = ((f32[128,4,128]{2,0,1:T(8,128)}), f32[128,4,128]{2,0,1:T(8,128)S(1)}, u32[]{:S(2)}, u32[]{:S(2)}) async-start(f32[128,4,128]{2,0,1:T(8,128)} %copy.74), calls=%async_computation.23 | async-start | bytes 524288 | tf_op jit(solution)/shard_map/all_to_all | solution.py:57
  548.1 13.7 %all-to-all-start.23 = ((f32[128,4,128]{2,0,1:T(8,128)}), f32[128,4,128]{2,0,1:T(8,128)S(1)}, u32[]{:S(2)}, u32[]{:S(2)}) async-start(f32[128,4,128]{2,0,1:T(8,128)} %copy.76), calls=%async_computation.25 | async-start | bytes 524288 | tf_op jit(solution)/shard_map/all_to_all | solution.py:66
  584.7 22.0 %all-to-all-start.24 = ((f32[64,8,128]{2,1,0:T(8,128)}), f32[64,8,128]{2,1,0:T(8,128)S(1)}, u32[]{:S(2)}, u32[]{:S(2)}) async-start(f32[64,8,128]{2,1,0:T(8,128)} %fusion.39), calls=%async_computation.26 | async-start | bytes 524288 | tf_op jit(solution)/shard_map/all_to_all | solution.py:94
  606.7 25.6 %all-to-all-start.26 = ((f32[64,8,128]{2,1,0:T(8,128)}), f32[64,8,128]{2,1,0:T(8,128)S(1)}, u32[]{:S(2)}, u32[]{:S(2)}) async-start(f32[64,8,128]{2,1,0:T(8,128)} %fusion.38), calls=%async_computation.28 | async-start | bytes 524288 | tf_op jit(solution)/shard_map/all_to_all | solution.py:101
  632.3 13.7 %all-to-all-start.25 = ((f32[4,2,8192]{2,1,0:T(2,128)}), f32[4,2,8192]{2,1,0:T(2,128)S(1)}, u32[]{:S(2)}, u32[]{:S(2)}) async-start(f32[4,2,8192]{2,1,0:T(2,128)} %all_to_all.435), calls=%async_computation.27 | async-start | bytes 524288 | tf_op jit(solution)/shard_map/all_to_all | solution.py:93
  646.0 9.8 %all-to-all-start.27 = ((f32[4,2,8192]{2,1,0:T(2,128)}), f32[4,2,8192]{2,1,0:T(2,128)S(1)}, u32[]{:S(2)}, u32[]{:S(2)}) async-start(f32[4,2,8192]{2,1,0:T(2,128)} %all_to_all.441), calls=%async_computation.29 | async-start | bytes 524288 | tf_op jit(solution)/shard_map/all_to_all | solution.py:100
  (9 other events, 91.9 us)
Sparse Core Ops, SparseCore 0:
  142.3 35.9 reduce-scatter.2
  181.1 31.8 reduce-scatter.4
where the time goes:
time: 680 us; the launch traced here: 669 us
  matrix products  212 us (31%)
  starting transfers between devices  196 us (29%)
  waiting for transfers between devices  183 us (27%)
  local copies, waits for them, and re-layouts  28.4 us (4%)
  blocking collectives  25.5 us (4%)
  between operations  15.6 us (2%)
  other arithmetic  7.45 us (1%)
    dot_general x70, matrix products, contract(): jnp.einsum(form, operand, table, precision=HIGHEST, preferred_element_typ...  201 us
    all_to_all x4, waiting for transfers between devices, to_grid(): lax.all_to_all(second_real.reshape(row_count, GU), 'tile', split_axis=1,...  46.7 us
    all_to_all x4, starting transfers between devices, to_grid(): lax.all_to_all(second_real.reshape(row_count, GU), 'tile', split_axis=1,...  43.6 us
    all_to_all x3, waiting for transfers between devices, to_image(): lax.all_to_all(line_imag, 'tile', split_axis=0, concat_axis=1, tiled=True)  38.7 us
    all_to_all x3, starting transfers between devices, to_image(): lax.all_to_all(line_imag, 'tile', split_axis=0, concat_axis=1, tiled=True)  35.5 us
    all_to_all x4, waiting for transfers between devices, to_grid(): lax.all_to_all(second_imag.reshape(row_count, GU), 'tile', split_axis=1,...  28.9 us
    all_to_all x3, starting transfers between devices, to_image(): lax.all_to_all(line_real, 'tile', split_axis=0, concat_axis=1, tiled=True)  27.4 us
    reduce_scatter x1, waiting for transfers between devices, shards(): lax.psum_scatter(part_imag, 'vis', scatter_dimension=1, tiled=True)  24 us
  transfers between devices with their start and end apart: 30, of which 23 were waited for; matrix products, arithmetic and copies ran while one was open for 22% of the time, Pallas kernels for 0%

commit v1 on v0

v1 whole, which is shorter than its diff:
```python
import functools
import math

import jax
import jax.numpy as jnp
import numpy as np
from jax import lax
from jax.experimental import pallas as pl
from jax.experimental.pallas import tpu as pltpu
from jax.sharding import PartitionSpec as P

GU = 32768
GV = 512
UVT = 128
CAP = 256
N_TILE = 64
N_VIS = 4
BLOCKS = N_TILE * N_VIS
WIDTH = GU // BLOCKS
HALO = 640
PHASES = 3
STEP_SIZE = 0.5
THRESHOLD = 0.05
JOINT = ("tile", "vis")
F32 = jnp.float32
BF16 = jnp.bfloat16
NN = (((1,), (0,)), ((), ()))
NT = (((1,), (1,)), ((), ()))
TN = (((0,), (0,)), ((), ()))
MIB = 1024 * 1024


def angles(left, right, length):
    return 2.0 * math.pi / length * ((np.asarray(left)[:, None] * np.asarray(right)[None, :]) % length)


def split_table(table, axis):
    table = np.asarray(table, np.float32)
    high = table.astype(jnp.bfloat16)
    low = (table - high.astype(np.float32)).astype(jnp.bfloat16)
    return np.concatenate([high, low], axis)


def block_owner():
    owner = []
    for run in range(16):
        x, y = run // 4, run % 4
        y = y if x % 2 == 0 else 3 - y
        for spot in range(8):
            z = spot if run % 2 == 0 else 7 - spot
            for core in range(2):
                owner.append((((x * 2 + z // 4) * 4 + y) * 2 + core) * 4 + z % 4)
    return owner


def build_tables():
    tables = {}
    scale = 1.0 / math.sqrt(GV * GU)
    first = angles(np.arange(256), np.arange(256), 256)
    second = angles(np.arange(128), np.arange(128), 128)
    cosine, sine = np.cos(second), np.sin(second)
    twiddle = angles(np.arange(128), np.arange(256), GU)
    tables["row_twiddle"] = (np.stack([np.cos(twiddle), -np.sin(twiddle)]) * scale).astype(np.float32)
    half = angles([1], np.arange(128), 256)
    tables["half_twiddle"] = np.concatenate([np.cos(half), np.sin(half)]).astype(np.float32)
    tables["back_first"] = split_table(np.concatenate([np.cos(first), np.sin(first)], 0), 1)
    tables["back_twiddle"] = np.stack([np.cos(twiddle.T), np.sin(twiddle.T)]).astype(np.float32)
    tables["back_second"] = split_table(np.concatenate([cosine, -sine], 1) * scale, 1)
    block = np.block([[cosine, -sine], [sine, cosine]])
    tables["point_right"] = split_table(block, 0)
    tables["point_left"] = split_table(block.T, 1)
    tables["point_back"] = split_table(block, 1)
    quarter = angles(np.arange(4), np.arange(128), GV)
    tables["lane_twiddle"] = np.stack([np.cos(quarter), np.sin(quarter)], 1).astype(np.float32)
    rows = np.stack([np.cos(quarter[1:]), np.sin(quarter[1:])], 1)[:, :, :, None]
    tables["side_twiddle"] = np.broadcast_to(rows, (3, 2, 128, 128)).astype(np.float32)
    window = angles(np.arange(PHASES), np.arange(128), HALO)
    tables["window_twiddle"] = np.stack([np.cos(window), np.sin(window)], 1).astype(np.float32)
    back = []
    for phase in range(PHASES):
        share = (1.0 if phase == 0 else 2.0) / (GV * HALO)
        turn = angles(5 * np.arange(128) + phase, 256 + np.arange(128), HALO)
        back.append(split_table(np.concatenate([np.cos(turn), -np.sin(turn)], 0) * share, 0))
    tables["window_back"] = np.stack(back)
    return tables


TABLES = build_tables()
OWNER = block_owner()


def window_turns():
    place = np.array([3, 4, 0, 1])
    out = np.zeros((N_VIS, PHASES, N_VIS, 2), np.float32)
    for at in range(N_VIS):
        for phase in range(PHASES):
            for block in range(N_VIS):
                turn = 2.0 * math.pi * (place[(at + block) % N_VIS] * phase % 5) / 5.0
                out[at, phase, block] = (math.cos(turn), math.sin(turn))
    return out.reshape(N_VIS, -1)


def dot(left, right, dims=NN):
    return lax.dot_general(left, right, dims, preferred_element_type=F32)


def parts(value, axis):
    high = value.astype(BF16)
    low = (value - high.astype(F32)).astype(BF16)
    return jnp.concatenate([high, low, high], axis=axis)


def both(table, axis):
    high, low = jnp.split(table[...], 2, axis=axis)
    return jnp.concatenate([high, high, low], axis=axis)


def twice(value, axis):
    return jnp.concatenate([value, value], axis=axis)


def call(kernel, outs, *args, smem=(), scratch=(), flops=0, vmem=32):
    specs = [
        pl.BlockSpec(memory_space=pltpu.SMEM if at in smem else pltpu.VMEM) for at in range(len(args))
    ]
    size = sum(int(np.prod(a.shape)) * a.dtype.itemsize for a in args)
    size += sum(int(np.prod(o.shape)) * o.dtype.itemsize for o in outs)
    return pl.pallas_call(
        kernel,
        out_shape=outs,
        in_specs=specs,
        out_specs=[pl.BlockSpec(memory_space=pltpu.VMEM)] * len(outs),
        scratch_shapes=list(scratch),
        compiler_params=pltpu.CompilerParams(vmem_limit_bytes=vmem * MIB),
        cost_estimate=pl.CostEstimate(flops=flops, bytes_accessed=size, transcendentals=0),
    )(*args)


def shape(dims, dtype):
    return jax.ShapeDtypeStruct(dims, dtype)


def cross_forward(blocks):
    (r0, i0), (r1, i1), (r2, i2), (r3, i3) = blocks
    ar, ai, br, bi = r0 + r2, i0 + i2, r0 - r2, i0 - i2
    cr, ci, dr, di = r1 + r3, i1 + i3, r1 - r3, i1 - i3
    return [(ar + cr, ai + ci), (br + di, bi - dr), (ar - cr, ai - ci), (br - di, bi + dr)]


def cross_back(blocks):
    (r0, i0), (r1, i1), (r2, i2), (r3, i3) = blocks
    ar, ai, br, bi = r0 + r2, i0 + i2, r0 - r2, i0 - i2
    cr, ci, dr, di = r1 + r3, i1 + i3, r1 - r3, i1 - i3
    return [(ar + cr, ai + ci), (br - di, bi + dr), (ar - cr, ai - ci), (br + di, bi - dr)]


def turn_forward(real, imag, cosine, sine):
    return real * cosine + imag * sine, imag * cosine - real * sine


def turn_back(real, imag, cosine, sine):
    return real * cosine - imag * sine, imag * cosine + real * sine


def row_kernel(sky_ref, psf_ref, right, half_turn, twiddle, left, out_ref, lines, send):
    for at in range(BLOCKS):
        piece = sky_ref[:, at * 128 : at * 128 + 128]
        lines[2 * at : 2 * at + 2, :] = piece
        row = 8 * OWNER[at] + 4
        send[row : row + 2, :] = piece
    for at in range(N_VIS):
        piece = psf_ref[:, at * 128 : at * 128 + 128]
        for tile in range(N_TILE):
            row = 8 * (tile * N_VIS + at) + 6
            send[row : row + 2, :] = piece
    pieces = [
        lines[pl.ds(2 * odd + row, 128, stride=4), :] for row in range(2) for odd in range(2)
    ]
    high, low = right[0:128, :], right[256:384, :]
    mixed = dot(parts(jnp.concatenate(pieces, 1), 0), jnp.concatenate([high, high, low], 0), TN)
    for row in range(2):
        even = mixed[row * 256 : row * 256 + 128]
        odd = mixed[row * 256 + 128 : row * 256 + 256]
        odd_real, odd_imag = turn_forward(odd[:, :128], odd[:, 128:], half_turn[0:1], half_turn[1:2])
        real = jnp.concatenate([even[:, :128] + odd_real, even[:, :128] - odd_real], axis=1)
        imag = jnp.concatenate([even[:, 128:] + odd_imag, even[:, 128:] - odd_imag], axis=1)
        turned = jnp.concatenate(
            [real * twiddle[0] - imag * twiddle[1], real * twiddle[1] + imag * twiddle[0]], axis=0
        )
        done = dot(both(left, 1), parts(turned, 0))
        for half in range(2):
            send[pl.ds(8 * half + row, 128, stride=16), :] = done[:128, half * 128 : half * 128 + 128]
            send[pl.ds(8 * half + 2 + row, 128, stride=16), :] = done[128:, half * 128 : half * 128 + 128]
    out_ref[...] = send[...].astype(BF16)


def weight_kernel(taps_ref, visit_ref, row_ref, col_ref):
    taps_table = taps_ref[...]
    place = lax.broadcasted_iota(jnp.int32, (UVT, CAP), 0).astype(F32)

    def weights(offset, row):
        choose = jnp.where(place == row, 1.0, 0.0).astype(BF16)
        taps = dot(taps_table, choose)
        within = place - offset
        out = jnp.zeros((UVT, CAP), F32)
        for shift in range(8):
            out = jnp.where(within == float(shift), taps[shift : shift + 1, :], out)
        return out.astype(BF16)

    def pair(group, carry):
        for side in range(2):
            at = 2 * group + side
            entry = visit_ref[at]
            row_ref[at] = weights(entry[2:3], entry[4:5])
            col_ref[at] = weights(entry[3:4], entry[5:6])
        return carry

    lax.fori_loop(0, visit_ref.shape[0] // 2, pair, 0)


def uv_kernel(
    tile_ref, got_ref, visit_ref, row_ref, col_ref, right, back, twiddle, out_ref, base_ref, psf_ref,
    move, grid, resid, side,
):
    move[...] = got_ref[...].astype(F32)
    for slot, ref in ((4, base_ref), (6, psf_ref)):
        for row in range(2):
            side[pl.ds(row, 256, stride=2), :] = move[pl.ds(slot + row, 256, stride=8), :]
        ref[...] = side[...].astype(BF16)
    lines = []
    for rho in range(4):
        row = 8 * (rho // 2) + rho % 2
        lines.append(
            jnp.concatenate(
                [move[pl.ds(row, 128, stride=16), :], move[pl.ds(row + 2, 128, stride=16), :]], 0
            )
        )
    lines = jnp.concatenate(lines, axis=1).astype(BF16)
    mixed = dot(twice(lines, 0), right[...], TN)
    blocks = []
    for rho in range(4):
        real, imag = mixed[rho * 128 : rho * 128 + 128, :128], mixed[rho * 128 : rho * 128 + 128, 128:]
        if rho > 0:
            real, imag = turn_forward(real, imag, twiddle[rho, 0:1], twiddle[rho, 1:2])
        blocks.append((real, imag))
    for at, (real, imag) in enumerate(cross_forward(blocks)):
        grid[0:128, at * 128 : at * 128 + 128] = real.astype(BF16)
        grid[128:256, at * 128 : at * 128 + 128] = imag.astype(BF16)
    resid[...] = jnp.zeros_like(resid)

    def some(group, carry):
        for side in range(4):
            at = 4 * group + side
            start = pl.multiple_of(tile_ref[at] * UVT, UVT)
            entry = visit_ref[at]
            weight_row = row_ref[at]
            weight_col = col_ref[at].astype(F32)
            partial = dot(grid[:, pl.ds(start, UVT)], weight_row)
            model_real = jnp.sum(partial[:UVT] * weight_col, axis=0, keepdims=True)
            model_imag = jnp.sum(partial[UVT:] * weight_col, axis=0, keepdims=True)
            live = entry[6:7] > 0.5
            real = jnp.where(live, entry[0:1] - model_real, 0.0)
            imag = jnp.where(live, entry[1:2] - model_imag, 0.0)
            spread = jnp.concatenate([real * weight_col, imag * weight_col], axis=0).astype(BF16)
            resid[:, pl.ds(start, UVT)] += dot(spread, weight_row, NT)
        return carry

    lax.fori_loop(0, visit_ref.shape[0] // 4, some, 0)
    blocks = [
        (resid[0:128, at * 128 : at * 128 + 128], resid[128:256, at * 128 : at * 128 + 128])
        for at in range(4)
    ]
    turned = []
    for rho, (real, imag) in enumerate(cross_back(blocks)):
        if rho > 0:
            real, imag = turn_back(real, imag, twiddle[rho, 0:1], twiddle[rho, 1:2])
        turned.append(jnp.concatenate([real, imag], axis=1))
    done = dot(both(back, 1), parts(jnp.concatenate(turned, axis=0), 1), NT)
    for rho in range(4):
        row = 4 * (rho // 2) + rho % 2
        move[pl.ds(row, 128, stride=8), :] = done[:128, rho * 128 : rho * 128 + 128]
        move[pl.ds(row + 2, 128, stride=8), :] = done[128:, rho * 128 : rho * 128 + 128]
    out_ref[...] = move[0:1024, :].astype(BF16)


def back_kernel(got_ref, first, twiddle, second, out_ref, send_ref, move, send):
    move[...] = got_ref[...].astype(F32)
    lines = jnp.concatenate([move[pl.ds(slot, 256, stride=4), :] for slot in range(4)], 1).astype(BF16)
    mixed = dot(first[...], twice(lines, 0))
    for row in range(2):
        at = row * 128
        real = mixed[:256, at : at + 128] - mixed[256:, 256 + at : 384 + at]
        imag = mixed[256:, at : at + 128] + mixed[:256, 256 + at : 384 + at]
        turned = jnp.concatenate(
            [real * twiddle[0] - imag * twiddle[1], real * twiddle[1] + imag * twiddle[0]], axis=1
        )
        done = dot(both(second, 1), parts(turned, 1), NT)
        for half in range(2):
            move[pl.ds(2 * half + row, 128, stride=4), :] = done[:, half * 128 : half * 128 + 128]
    for at in range(BLOCKS):
        piece = move[2 * at : 2 * at + 2, :]
        out_ref[:, at * 128 : at * 128 + 128] = piece
        send[2 * OWNER[at] : 2 * OWNER[at] + 2, :] = piece
    send_ref[...] = send[...].astype(BF16)


def gather_window(blocks, phase):
    real, imag = None, None
    for at, value in enumerate(blocks):
        angle = 2.0 * math.pi * (at * phase % 5) / 5.0
        term = value * math.cos(angle) if at * phase % 5 else value
        real = term if real is None else real + term
        if at * phase % 5:
            term = value * -math.sin(angle)
            imag = term if imag is None else imag + term
    return real, imag


def to_frequency(real, imag, phase, window, side, right, left):
    if phase == 0:
        lines = parts(real, 1)
        table = jnp.concatenate([right[0:128, :], right[0:128, :], right[256:384, :]], axis=0)
    else:
        real, imag = turn_forward(real, imag, window[phase, 0:1], window[phase, 1:2])
        lines = parts(jnp.concatenate([real, imag], axis=1), 1)
        table = both(right, 0)
    mixed = dot(lines, table)
    quarters = [
        (mixed[at * 128 : at * 128 + 128, :128], mixed[at * 128 : at * 128 + 128, 128:])
        for at in range(4)
    ]
    turned = []
    for at, (real, imag) in enumerate(cross_forward(quarters)):
        if at > 0:
            real, imag = turn_forward(real, imag, side[at - 1, 0], side[at - 1, 1])
        turned.append(jnp.concatenate([real, imag], axis=0))
    done = dot(both(left, 1), parts(jnp.concatenate(turned, axis=1), 0))
    return done[:128], done[128:]


def transfer_kernel(turn_ref, *refs):
    blocks = [ref[...].astype(F32) for ref in refs[:N_VIS]]
    window, side, right, left, out_ref = refs[N_VIS:]
    for phase in range(PHASES):
        real, imag = None, None
        for at, value in enumerate(blocks):
            place = 2 * (phase * N_VIS + at)
            term = value * turn_ref[place] if phase else value
            real = term if real is None else real + term
            if phase:
                term = value * turn_ref[place + 1]
                imag = -term if imag is None else imag - term
        out_ref[phase, 0], out_ref[phase, 1] = to_frequency(
            real, imag, phase, window, side, right, left
        )


def conv_kernel(
    first, far_left, near_left, own, near_right, far_right, transfer, window, side, right, left,
    back, window_back, sky_ref, resid_ref, base_ref, *out_refs,
):
    blocks = [
        ref[...].astype(F32) for ref in (far_left, near_left, own, near_right, far_right)
    ]
    total = jnp.zeros((GV, 128), F32)
    for phase in range(PHASES):
        real, imag = gather_window(blocks, phase)
        real, imag = to_frequency(real, imag, phase, window, side, right, left)
        trans_real, trans_imag = transfer[phase, 0], transfer[phase, 1]
        blur = jnp.concatenate(
            [real * trans_real - imag * trans_imag, real * trans_imag + imag * trans_real], axis=0
        )
        mixed = dot(both(back, 1), parts(blur, 0))
        quarters = []
        for at in range(4):
            real, imag = mixed[:128, at * 128 : at * 128 + 128], mixed[128:, at * 128 : at * 128 + 128]
            if at > 0:
                real, imag = turn_back(real, imag, side[at - 1, 0], side[at - 1, 1])
            quarters.append((real, imag))
        lines = [jnp.concatenate([real, imag], axis=1) for real, imag in cross_back(quarters)]
        high, low = window_back[phase, 0:256], window_back[phase, 256:512]
        table = jnp.concatenate([high, high, low], axis=0)
        total = total + dot(parts(jnp.concatenate(lines, axis=0), 1), table)
    resid = resid_ref[...].astype(F32)
    base = base_ref[...].astype(F32)
    sky = step(base, resid) if first else sky_ref[...]
    sky = step(sky, resid - total)
    if first:
        out_refs[0][...] = sky
        out_refs[1][...] = (sky - base).astype(BF16)
    else:
        out_refs[0][...] = sky.astype(BF16)


def step(sky, gradient):
    moved = sky + STEP_SIZE * gradient
    return moved - jnp.clip(moved, -THRESHOLD, THRESHOLD)


def last_kernel(got_ref, out_ref, move):
    move[...] = got_ref[...].astype(F32)
    for at in range(BLOCKS):
        out_ref[:, at * 128 : at * 128 + 128] = move[2 * OWNER[at] : 2 * OWNER[at] + 2, :]


def exchange(rows):
    blocks = rows.reshape(BLOCKS, rows.shape[0] // BLOCKS, 128)
    return lax.all_to_all(blocks, JOINT, 0, 0, tiled=True).reshape(rows.shape)


def halo(block, step):
    pairs = [(OWNER[at], OWNER[(at + step) % BLOCKS]) for at in range(BLOCKS)]
    return lax.ppermute(block, JOINT, pairs)


def around_vis(value, step):
    return lax.ppermute(value, "vis", [(at, (at + step) % N_VIS) for at in range(N_VIS)])


def shards(
    model_image, psf, kernel_table, observed, visit_tile, visit_count, cell_offset, kernel_row
):
    at_vis = lax.axis_index("vis")
    tables = TABLES

    live = jnp.arange(CAP)[None, :] < visit_count[0][:, None]
    tile_row = jnp.broadcast_to((visit_tile[0] % 4)[:, None], live.shape)
    packed = jnp.stack(
        [
            observed[0, 0],
            observed[1, 0],
            cell_offset[0, 0].astype(F32),
            cell_offset[1, 0].astype(F32),
            kernel_row[0, 0].astype(F32),
            kernel_row[1, 0].astype(F32),
            live.astype(F32),
            tile_row.astype(F32),
        ],
        axis=1,
    )
    pieces = [lax.dynamic_slice_in_dim(packed, at_vis * 4, 4, 0)]
    for hop in range(1, N_VIS):
        group = lax.dynamic_slice_in_dim(packed, (at_vis + hop) % N_VIS * 4, 4, 0)
        pieces.append(around_vis(group, hop))
    visits = jnp.concatenate(pieces, axis=0)

    send = call(
        row_kernel,
        [shape((8 * BLOCKS, 128), BF16)],
        model_image,
        psf,
        tables["point_right"],
        tables["half_twiddle"],
        tables["row_twiddle"],
        tables["point_left"],
        vmem=60,
        scratch=[pltpu.VMEM((512, 128), F32), pltpu.VMEM((8 * BLOCKS, 128), F32)],
        flops=2 * 3 * 256 * 256 * 1024,
    )[0]
    got = exchange(send)
    visit_rows = visits[:, 7, 0].astype(jnp.int32)
    taps = jnp.pad(kernel_table.astype(BF16).T, ((0, 8), (0, 0)))
    weight_row, weight_col = call(
        weight_kernel,
        [shape((16, UVT, CAP), BF16), shape((16, UVT, CAP), BF16)],
        taps,
        visits,
        flops=2 * 16 * 2 * 16 * 128 * 256 * 64,
    )

    send, base, quarter = call(
        uv_kernel,
        [shape((4 * BLOCKS, 128), BF16), shape((GV, 128), BF16), shape((GV, 128), BF16)],
        visit_rows,
        got,
        visits,
        weight_row,
        weight_col,
        tables["point_right"],
        tables["point_back"],
        tables["lane_twiddle"],
        smem=(0,),
        scratch=[
            pltpu.VMEM((8 * BLOCKS, 128), F32),
            pltpu.VMEM((256, GV), BF16),
            pltpu.VMEM((256, GV), F32),
            pltpu.VMEM((GV, 128), F32),
        ],
        flops=2 * 7 * 256 * 512 * 512,
    )
    got = exchange(send)
    transfer = call(
        transfer_kernel,
        [shape((PHASES, 2, 128, 4 * 128), F32)],
        lax.dynamic_index_in_dim(jnp.asarray(window_turns()), at_vis, 0, keepdims=False),
        quarter,
        *[around_vis(quarter, N_VIS - hop) for hop in range(1, N_VIS)],
        tables["window_twiddle"],
        tables["side_twiddle"],
        tables["point_right"],
        tables["point_left"],
        smem=(0,),
        flops=2 * PHASES * 3 * 2 * 512 * 256 * 256,
    )[0]
    residual_image, send = call(
        back_kernel,
        [shape((2, GU), F32), shape((2 * BLOCKS, 128), BF16)],
        got,
        tables["back_first"],
        tables["back_twiddle"],
        tables["back_second"],
        scratch=[pltpu.VMEM((4 * BLOCKS, 128), F32), pltpu.VMEM((2 * BLOCKS, 128), F32)],
        flops=2 * 3 * 512 * 512 * 256,
    )

    resid = exchange(send)
    wide = base.astype(F32)
    change = (step(wide, resid.astype(F32)) - wide).astype(BF16)
    sky = wide
    for turn in range(2):
        first = turn == 0
        outs = [shape((GV, 128), F32), shape((GV, 128), BF16)] if first else [shape((GV, 128), BF16)]
        got = call(
            functools.partial(conv_kernel, first),
            outs,
            halo(change, 2),
            halo(change, 1),
            change,
            halo(change, -1),
            halo(change, -2),
            transfer,
            tables["window_twiddle"],
            tables["side_twiddle"],
            tables["point_right"],
            tables["point_left"],
            tables["point_back"],
            tables["window_back"],
            base if first else sky,
            resid,
            base,
            flops=2 * PHASES * 3 * 4 * 512 * 256 * 256,
        )
        if first:
            sky, change = got
    got = exchange(got[0])
    model_next = call(
        last_kernel, [shape((2, GU), F32)], got, scratch=[pltpu.VMEM((2 * BLOCKS, 128), F32)]
    )[0]
    return (model_next, residual_image)


def solution(mesh):
    placed = (
        P(("tile", "vis"), None),
        P(("tile", "vis"), None),
        P(),
        P(None, "vis", "tile", None),
        P("vis", "tile"),
        P("vis", "tile"),
        P(None, "vis", "tile", None),
        P(None, "vis", "tile", None),
    )
    return jax.shard_map(
        shards,
        mesh=mesh,
        in_specs=placed,
        out_specs=(P(("tile", "vis"), None), P(("tile", "vis"), None)),
        check_vma=False,
    )
```

time: 680 us -> 145 us (0.21); the launches traced: 669 us -> 145 us
  matrix products: 212 us -> 0 us
  starting transfers between devices: 196 us -> 37.2 us
  waiting for transfers between devices: 183 us -> 27.9 us
  Pallas kernels: 0 us -> 25.2 us
  local copies, waits for them, and re-layouts: 28.4 us -> 3.38 us
  blocking collectives: 25.5 us -> 49.7 us
  between operations: 15.6 us -> 1.02 us
  other arithmetic: 7.45 us -> 0.57 us
    dot_general x75 -> x0, matrix products: 212 us -> none  [the longest x70 201 us: contract(): jnp.einsum(form, operand, table, precision=HIGHEST, preferred_element_typ...]
    all_to_all x28 -> x2, starting transfers between devices: 196 us -> 21.1 us  [exchange(): return lax.all_to_all(blocks, JOINT, 0, 0, tiled=True).reshape(rows.shape)]
    all_to_all x28 -> x2, waiting for transfers between devices: 159 us -> 8.84 us  [exchange(): return lax.all_to_all(blocks, JOINT, 0, 0, tiled=True).reshape(rows.shape)]
    all_to_all x0 -> x2, blocking collectives: none -> 49.7 us  [exchange(): return lax.all_to_all(blocks, JOINT, 0, 0, tiled=True).reshape(rows.shape)]
    all_gather x2 -> x0, blocking collectives: 25.5 us -> none  [the longest x1 13 us: shards(): lax.all_gather(grid_real, 'vis', axis=1, tiled=True)]
    pallas_call x0 -> x8, Pallas kernels: none -> 25.2 us  [call(): pl.pallas_call(kernel, out_shape=outs, in_specs=specs, out_specs=[pl.Bloc...]
    reduce_scatter x2 -> x0, waiting for transfers between devices: 24 us -> none  [the longest x1 24 us: shards(): lax.psum_scatter(part_imag, 'vis', scatter_dimension=1, tiled=True)]
    all_to_all x50 -> x0, local copies, waits for them, and re-layouts: 22.3 us -> none  [the longest x8 4.1 us: to_grid(): lax.all_to_all(second_real.reshape(row_count, GU), 'tile', split_axis=1,...]
  transfers between devices with their start and end apart: 30 -> 16, of which waited for: 23 -> 10; matrix products, arithmetic and copies ran while one was open for 22% -> 1% of each run, Pallas kernels for 0% -> 4%
where the time goes in v1:
time: 145 us
  blocking collectives  49.7 us (34%)
  starting transfers between devices  37.2 us (26%)
  waiting for transfers between devices  27.9 us (19%)
  Pallas kernels  25.2 us (17%)
  local copies, waits for them, and re-layouts  3.38 us (2%)
    all_to_all x2, blocking collectives, exchange(): return lax.all_to_all(blocks, JOINT, 0, 0, tiled=True).reshape(rows.shape)  49.7 us
    pallas_call x8, Pallas kernels, call(): pl.pallas_call(kernel, out_shape=outs, in_specs=specs, out_specs=[pl.Bloc...  25.2 us
    all_to_all x2, starting transfers between devices, exchange(): return lax.all_to_all(blocks, JOINT, 0, 0, tiled=True).reshape(rows.shape)  21.1 us
    ppermute x6, waiting for transfers between devices, around_vis(): lax.ppermute(value, 'vis', [(at, (at + step) % N_VIS) for at in range(N_V...  10.6 us
    ppermute x6, starting transfers between devices, around_vis(): lax.ppermute(value, 'vis', [(at, (at + step) % N_VIS) for at in range(N_V...  9.56 us
    all_to_all x2, waiting for transfers between devices, exchange(): return lax.all_to_all(blocks, JOINT, 0, 0, tiled=True).reshape(rows.shape)  8.84 us
    ppermute x8, waiting for transfers between devices, halo(): return lax.ppermute(block, JOINT, pairs)  8.42 us
    ppermute x8, starting transfers between devices, halo(): return lax.ppermute(block, JOINT, pairs)  6.58 us
  transfers between devices with their start and end apart: 16, of which 10 were waited for; matrix products, arithmetic and copies ran while one was open for 1% of the time, Pallas kernels for 4%

profile of v1, /device:TPU:1, one launch (start us, length us, event | category | flops | bytes accessed | tf_op | source)
XLA Modules:
  0.0 145.0 jit_solution(106659999945852144)
XLA Ops:
  0.7 3.2 %shard_map.212 = bf16[2048,128]{1,0:T(8,128)(2,1)} custom-call(f32[2,32768]{1,0:T(2,128)} %sky_ref.1, f32[2,512]{1,0:T(2,128)} %psf_ref.1, bf16[512,256]{1,0:T(8,128)(2,1)} %constant.79.clone.right.refs_6_, f32[2,128]{1,0:T(2,128)} %constant.80.clone.half_turn, f32[2,128,256]{2,1,0:T(8,128)} %constant.81.clone.twiddle, ...), custom_call_target="tpu_custom_call" | custom-call | flops 402653184 | bytes 1577984 | tf_op jit(solution)/shard_map/pallas_call | solution.py:128
  3.9 15.7 %all-to-all-start = ((bf16[256,8,128]{2,1,0:T(8,128)(2,1)}), bf16[256,8,128]{2,1,0:T(8,128)(2,1)S(1)}, u32[]{:S(2)}, u32[]{:S(2)}) async-start(bf16[256,8,128]{2,1,0:T(8,128)(2,1)} %bitcast.35), calls=%async_computation | async-start | bytes 1048576 | tf_op jit(solution)/shard_map/all_to_all | solution.py:408
  20.3 3.9 %collective-permute-start.2 = (f32[4,8,256]{2,1,0:T(8,128)S(1)}, f32[4,8,256]{2,1,0:T(8,128)S(1)}, u32[]{:S(2)}, u32[]{:S(2)}) collective-permute-start(f32[4,8,256]{2,1,0:T(8,128)S(1)} %get-tuple-element.21), channel_id=1, source_target_pairs={{0,3},{1,0},{2,1},{3,2},{4,7},{5,4},{6,5},{7,6},{8,11},{9,8},{10,9... | collective-permute-start | bytes 98312 | tf_op jit(solution)/shard_map/ppermute | solution.py:417
  24.6 7.2 %collective-permute-done.2 = f32[4,8,256]{2,1,0:T(8,128)S(1)} collective-permute-done((f32[4,8,256]{2,1,0:T(8,128)S(1)}, f32[4,8,256]{2,1,0:T(8,128)S(1)}, u32[]{:S(2)}, u32[]{:S(2)}) %collective-permute-start.2) | collective-permute-done | bytes 32800 | tf_op jit(solution)/shard_map/ppermute | solution.py:417
  31.8 1.7 %collective-permute-done.1 = f32[4,8,256]{2,1,0:T(8,128)S(1)} collective-permute-done((f32[4,8,256]{2,1,0:T(8,128)S(1)}, f32[4,8,256]{2,1,0:T(8,128)S(1)}, u32[]{:S(2)}, u32[]{:S(2)}) %collective-permute-start.1) | collective-permute-done | bytes 32800 | tf_op jit(solution)/shard_map/ppermute | solution.py:417
  33.5 1.7 %collective-permute-done = f32[4,8,256]{2,1,0:T(8,128)S(1)} collective-permute-done((f32[4,8,256]{2,1,0:T(8,128)S(1)}, f32[4,8,256]{2,1,0:T(8,128)S(1)}, u32[]{:S(2)}, u32[]{:S(2)}) %collective-permute-start) | collective-permute-done | bytes 32800 | tf_op jit(solution)/shard_map/ppermute | solution.py:417
  35.6 3.5 %shard_map.213 = (bf16[16,128,256]{2,1,0:T(8,128)(2,1)S(1)}, bf16[16,128,256]{2,1,0:T(8,128)(2,1)S(1)}) custom-call(bf16[16,128]{1,0:T(8,128)(2,1)S(1)} %pad.4.taps_ref, f32[16,8,256]{2,1,0:T(8,128)S(1)} %pad_maximum_fusion.visit_ref), custom_call_target="tpu_custom_call" | custom-call | flops 2147483648 | bytes 2232320 | tf_op jit(solution)/shard_map/pallas_call | solution.py:128
  39.2 1.0 copy-done.10
  40.2 0.9 all-to-all-done
  41.1 1.2 copy-done.11
  42.3 4.0 %shard_map.214 = (bf16[1024,128]{1,0:T(8,128)(2,1)S(1)}, bf16[512,128]{1,0:T(8,128)(2,1)S(1)}, bf16[512,128]{1,0:T(8,128)(2,1)S(1)}) custom-call(s32[16]{0:T(128)S(1)} %fusion.1.tile_ref, bf16[2048,128]{1,0:T(8,128)(2,1)S(1)} %bitcast.31, f32[16,8,256]{2,1,0:T(8,128)S(1)} %pad_maximum_fusion.visit_ref, bf16[16,128,256]{2,1,0:T(8,128)(2,1)S(1)} %get-tuple-element.11.row_ref, ...), custom_call_target="tpu_custom_call" | custom-call | flops 939524096 | bytes 3805248 | tf_op jit(solution)/shard_map/pallas_call | solution.py:128
  46.3 26.7 %all_to_all.20 = bf16[256,4,128]{2,1,0:T(4,128)(2,1)S(1)} all-to-all(bf16[256,4,128]{2,1,0:T(4,128)(2,1)S(1)} %bitcast.32), channel_id=1, replica_groups=mesh['tile'=64,'vis'=4] {'tile','vis'}, dimensions={0} | all-to-all | bytes 524288 | tf_op jit(solution)/shard_map/all_to_all | solution.py:408
  73.0 2.0 %shard_map.215 = (f32[2,32768]{1,0:T(2,128)}, bf16[512,128]{1,0:T(8,128)(2,1)}) custom-call(bf16[1024,128]{1,0:T(8,128)(2,1)S(1)} %bitcast.33, bf16[512,512]{1,0:T(8,128)(2,1)S(1)} %copy-done.2, f32[2,256,128]{2,1,0:T(8,128)S(1)} %copy-done.6, bf16[128,512]{1,0:T(8,128)(2,1)S(1)} %copy-done.7), custom_call_target="tpu_custom_call" | custom-call | flops 402653184 | bytes 1572864 | tf_op jit(solution)/shard_map/pallas_call | solution.py:128
  75.0 5.4 %all-to-all-start.2 = ((bf16[256,2,128]{2,1,0:T(2,128)(2,1)}), bf16[256,2,128]{2,1,0:T(2,128)(2,1)S(1)}, u32[]{:S(2)}, u32[]{:S(2)}) async-start(bf16[256,2,128]{2,1,0:T(2,128)(2,1)} %bitcast.13), calls=%async_computation.2 | async-start | bytes 262144 | tf_op jit(solution)/shard_map/all_to_all | solution.py:408
  80.5 1.7 %collective-permute-start.9 = (bf16[512,128]{1,0:T(8,128)(2,1)S(1)}, bf16[512,128]{1,0:T(8,128)(2,1)S(1)}, u32[]{:S(2)}, u32[]{:S(2)}) collective-permute-start(bf16[512,128]{1,0:T(8,128)(2,1)S(1)} %get-tuple-element.16.refs_0_), channel_id=1, source_target_pairs={{0,1},{1,2},{2,3},{3,0},{4,5},{5,6},{6,7},{7,4},{8,9},{9,10},{10,1... | collective-permute-start | bytes 393224 | tf_op jit(solution)/shard_map/ppermute | solution.py:417
  82.2 2.6 %collective-permute-start.8 = (bf16[512,128]{1,0:T(8,128)(2,1)S(1)}, bf16[512,128]{1,0:T(8,128)(2,1)S(1)}, u32[]{:S(2)}, u32[]{:S(2)}) collective-permute-start(bf16[512,128]{1,0:T(8,128)(2,1)S(1)} %get-tuple-element.16.refs_0_), channel_id=1, source_target_pairs={{0,2},{1,3},{2,0},{3,1},{4,6},{5,7},{6,4},{7,5},{8,10},{9,11},{10,... | collective-permute-start | bytes 393224 | tf_op jit(solution)/shard_map/ppermute | solution.py:417
  84.8 0.9 collective-permute-start.7
  85.7 8.0 %all-to-all-done.2 = bf16[256,2,128]{2,1,0:T(2,128)(2,1)S(1)} async-done(((bf16[256,2,128]{2,1,0:T(2,128)(2,1)}), bf16[256,2,128]{2,1,0:T(2,128)(2,1)S(1)}, u32[]{:S(2)}, u32[]{:S(2)}) %all-to-all-start.2) | async-done | bytes 131104 | tf_op jit(solution)/shard_map/all_to_all | solution.py:408
  93.8 0.9 collective-permute-start.6
  95.4 1.0 collective-permute-start.4
  97.8 2.8 %shard_map.216.transfer = f32[3,2,128,512]{3,2,1,0:T(8,128)S(1)} custom-call(f32[24]{0:T(128)S(1)} %fusion.2.turn_ref, bf16[512,128]{1,0:T(8,128)(2,1)S(1)} %get-tuple-element.16.refs_0_, bf16[512,128]{1,0:T(8,128)(2,1)S(1)} %collective-permute-done.7.refs_1_, bf16[512,128]{1,0:T(8,128)(2,1)S(1)} %collective-permute-done.8.refs_2_, ...), custom_call_target="tpu_custom_call" | custom-call | flops 1207959552 | bytes 3017824 | tf_op jit(solution)/shard_map/pallas_call | solution.py:128
  100.8 2.7 %collective-permute-done.3.far_left = bf16[512,128]{1,0:T(8,128)(2,1)S(1)} collective-permute-done((bf16[512,128]{1,0:T(8,128)(2,1)S(1)}, bf16[512,128]{1,0:T(8,128)(2,1)S(1)}, u32[]{:S(2)}, u32[]{:S(2)}) %collective-permute-start.3) | collective-permute-done | bytes 131104 | tf_op jit(solution)/shard_map/ppermute | solution.py:413
  103.5 4.4 %shard_map.217 = (f32[512,128]{1,0:T(8,128)S(1)}, bf16[512,128]{1,0:T(8,128)(2,1)S(1)}) custom-call(bf16[512,128]{1,0:T(8,128)(2,1)S(1)} %collective-permute-done.3.far_left, bf16[512,128]{1,0:T(8,128)(2,1)S(1)} %collective-permute-done.4.near_left, bf16[512,128]{1,0:T(8,128)(2,1)S(1)} %fusion.own, bf16[512,128]{1,0:T(8,128)(2,1)S(1)} %collective-permute-done.5.near_right, ...), custom_call_target="tpu_custom_call" | custom-call | flops 2415919104 | bytes 4590592 | tf_op jit(solution)/shard_map/pallas_call | solution.py:128
  108.2 0.9 collective-permute-start.12
  109.0 0.9 collective-permute-start.11
  109.9 1.3 collective-permute-start.10
  111.2 1.9 %collective-permute-done.13.far_right = bf16[512,128]{1,0:T(8,128)(2,1)S(1)} collective-permute-done((bf16[512,128]{1,0:T(8,128)(2,1)S(1)}, bf16[512,128]{1,0:T(8,128)(2,1)S(1)}, u32[]{:S(2)}, u32[]{:S(2)}) %collective-permute-start.13) | collective-permute-done | bytes 131104 | tf_op jit(solution)/shard_map/ppermute | solution.py:413
  113.1 1.8 %collective-permute-done.12.near_right = bf16[512,128]{1,0:T(8,128)(2,1)S(1)} collective-permute-done((bf16[512,128]{1,0:T(8,128)(2,1)S(1)}, bf16[512,128]{1,0:T(8,128)(2,1)S(1)}, u32[]{:S(2)}, u32[]{:S(2)}) %collective-permute-start.12) | collective-permute-done | bytes 131104 | tf_op jit(solution)/shard_map/ppermute | solution.py:413
  114.9 1.8 %collective-permute-done.10.far_left = bf16[512,128]{1,0:T(8,128)(2,1)S(1)} collective-permute-done((bf16[512,128]{1,0:T(8,128)(2,1)S(1)}, bf16[512,128]{1,0:T(8,128)(2,1)S(1)}, u32[]{:S(2)}, u32[]{:S(2)}) %collective-permute-start.10) | collective-permute-done | bytes 131104 | tf_op jit(solution)/shard_map/ppermute | solution.py:413
  116.8 4.4 %shard_map.218 = bf16[512,128]{1,0:T(8,128)(2,1)S(1)} custom-call(bf16[512,128]{1,0:T(8,128)(2,1)S(1)} %collective-permute-done.10.far_left, bf16[512,128]{1,0:T(8,128)(2,1)S(1)} %collective-permute-done.11.near_left, bf16[512,128]{1,0:T(8,128)(2,1)S(1)} %get-tuple-element.17.own, bf16[512,128]{1,0:T(8,128)(2,1)S(1)} %collective-permute-done.12.near_right, ...), custom_call_target="tpu_custom_call" | custom-call | flops 2415919104 | bytes 4459520 | tf_op jit(solution)/shard_map/pallas_call | solution.py:128
  121.2 23.0 %all_to_all.21 = bf16[256,2,128]{2,1,0:T(2,128)(2,1)S(1)} all-to-all(bf16[256,2,128]{2,1,0:T(2,128)(2,1)S(1)} %bitcast.34), channel_id=1, replica_groups=mesh['tile'=64,'vis'=4] {'tile','vis'}, dimensions={0} | all-to-all | bytes 262144 | tf_op jit(solution)/shard_map/all_to_all | solution.py:408
  144.2 0.8 shard_map.219
  (63 shorter events, 3.9 us)
Async XLA Ops:
  0.6 18.9 %copy-start.16 = (s32[1,16]{1,0:T(1,128)S(1)}, s32[1,16]{1,0:T(1,128)}, u32[]{:S(2)}) copy-start(s32[1,16]{1,0:T(1,128)} %param.26) | copy-start | bytes 196
  0.6 19.0 %copy-start.12 = (f32[2,1,16,256]{3,2,1,0:T(8,128)S(1)}, f32[2,1,16,256]{3,2,1,0:T(8,128)}, u32[]{:S(2)}) copy-start(f32[2,1,16,256]{3,2,1,0:T(8,128)} %param.24) | copy-start | bytes 98308
  0.7 19.0 %copy-start.13 = (s32[2,1,16,256]{3,2,1,0:T(8,128)S(1)}, s32[2,1,16,256]{3,2,1,0:T(8,128)}, u32[]{:S(2)}) copy-start(s32[2,1,16,256]{3,2,1,0:T(8,128)} %param.27) | copy-start | bytes 98308
  0.7 19.1 %copy-start.14 = (s32[2,1,16,256]{3,2,1,0:T(8,128)S(1)}, s32[2,1,16,256]{3,2,1,0:T(8,128)}, u32[]{:S(2)}) copy-start(s32[2,1,16,256]{3,2,1,0:T(8,128)} %param.28) | copy-start | bytes 98308
  0.7 19.2 %copy-start.17 = (s32[1,16]{1,0:T(1,128)S(1)}, s32[1,16]{1,0:T(1,128)}, u32[]{:S(2)}) copy-start(s32[1,16]{1,0:T(1,128)} %param.25) | copy-start | bytes 196
  0.7 23.9 %copy-start.15 = (f32[128,8]{0,1:T(8,128)S(1)}, f32[128,8]{0,1:T(8,128)}, u32[]{:S(2)}) copy-start(f32[128,8]{0,1:T(8,128)} %param.23) | copy-start | bytes 12292
  3.9 37.1 %all-to-all-start = ((bf16[256,8,128]{2,1,0:T(8,128)(2,1)}), bf16[256,8,128]{2,1,0:T(8,128)(2,1)S(1)}, u32[]{:S(2)}, u32[]{:S(2)}) async-start(bf16[256,8,128]{2,1,0:T(8,128)(2,1)} %bitcast.35), calls=%async_computation | async-start | bytes 1048576 | tf_op jit(solution)/shard_map/all_to_all | solution.py:408
  20.3 11.5 %collective-permute-start.2 = (f32[4,8,256]{2,1,0:T(8,128)S(1)}, f32[4,8,256]{2,1,0:T(8,128)S(1)}, u32[]{:S(2)}, u32[]{:S(2)}) collective-permute-start(f32[4,8,256]{2,1,0:T(8,128)S(1)} %get-tuple-element.21), channel_id=1, source_target_pairs={{0,3},{1,0},{2,1},{3,2},{4,7},{5,4},{6,5},{7,6},{8,11},{9,8},{10,9... | collective-permute-start | bytes 98312 | tf_op jit(solution)/shard_map/ppermute | solution.py:417
  24.2 9.4 %collective-permute-start.1 = (f32[4,8,256]{2,1,0:T(8,128)S(1)}, f32[4,8,256]{2,1,0:T(8,128)S(1)}, u32[]{:S(2)}, u32[]{:S(2)}) collective-permute-start(f32[4,8,256]{2,1,0:T(8,128)S(1)} %get-tuple-element.22), channel_id=1, source_target_pairs={{0,2},{1,3},{2,0},{3,1},{4,6},{5,7},{6,4},{7,5},{8,10},{9,11},{10,... | collective-permute-start | bytes 98312 | tf_op jit(solution)/shard_map/ppermute | solution.py:417
  24.2 11.0 %collective-permute-start = (f32[4,8,256]{2,1,0:T(8,128)S(1)}, f32[4,8,256]{2,1,0:T(8,128)S(1)}, u32[]{:S(2)}, u32[]{:S(2)}) collective-permute-start(f32[4,8,256]{2,1,0:T(8,128)S(1)} %get-tuple-element.23), channel_id=1, source_target_pairs={{0,1},{1,2},{2,3},{3,0},{4,5},{5,6},{6,7},{7,4},{8,9},{9,10},{10,1... | collective-permute-start | bytes 98312 | tf_op jit(solution)/shard_map/ppermute | solution.py:417
  35.6 5.4 %copy-start = (bf16[512,256]{1,0:T(8,128)(2,1)S(1)}, bf16[512,256]{1,0:T(8,128)(2,1)}, u32[]{:S(2)}) copy-start(bf16[512,256]{1,0:T(8,128)(2,1)} %constant.79.clone.right.refs_6_) | copy-start | bytes 786436
  35.6 5.4 %copy-start.5 = (bf16[256,512]{1,0:T(8,128)(2,1)S(1)}, bf16[256,512]{1,0:T(8,128)(2,1)}, u32[]{:S(2)}) copy-start(bf16[256,512]{1,0:T(8,128)(2,1)} %constant.83.clone.back) | copy-start | bytes 786436
  35.6 5.4 %copy-start.8 = (f32[4,2,128]{2,1,0:T(2,128)S(1)}, f32[4,2,128]{2,1,0:T(2,128)}, u32[]{:S(2)}) copy-start(f32[4,2,128]{2,1,0:T(2,128)} %constant.84.clone.twiddle) | copy-start | bytes 12292
  42.3 30.7 %copy-start.2 = (bf16[512,512]{1,0:T(8,128)(2,1)S(1)}, bf16[512,512]{1,0:T(8,128)(2,1)}, u32[]{:S(2)}) copy-start(bf16[512,512]{1,0:T(8,128)(2,1)} %constant.88.clone.first) | copy-start | bytes 1572868
  42.3 30.7 %copy-start.6 = (f32[2,256,128]{2,1,0:T(8,128)S(1)}, f32[2,256,128]{2,1,0:T(8,128)}, u32[]{:S(2)}) copy-start(f32[2,256,128]{2,1,0:T(8,128)} %constant.89.clone.twiddle) | copy-start | bytes 786436
  42.3 30.7 %copy-start.7 = (bf16[128,512]{1,0:T(8,128)(2,1)S(1)}, bf16[128,512]{1,0:T(8,128)(2,1)}, u32[]{:S(2)}) copy-start(bf16[128,512]{1,0:T(8,128)(2,1)} %constant.90.clone.second) | copy-start | bytes 393220
  46.2 51.5 %copy-start.1 = (bf16[256,512]{1,0:T(8,128)(2,1)S(1)}, bf16[256,512]{1,0:T(8,128)(2,1)}, u32[]{:S(2)}) copy-start(bf16[256,512]{1,0:T(8,128)(2,1)} %constant.82.clone.left.refs_7_) | copy-start | bytes 786436
  46.3 51.5 %copy-start.3 = (f32[3,2,128,128]{3,2,1,0:T(8,128)S(1)}, f32[3,2,128,128]{3,2,1,0:T(8,128)}, u32[]{:S(2)}) copy-start(f32[3,2,128,128]{3,2,1,0:T(8,128)} %constant.87.clone.refs_5_.side) | copy-start | bytes 1179652
  46.3 51.5 %copy-start.9 = (f32[3,2,128]{2,1,0:T(2,128)S(1)}, f32[3,2,128]{2,1,0:T(2,128)}, u32[]{:S(2)}) copy-start(f32[3,2,128]{2,1,0:T(2,128)} %constant.86.clone.refs_4_.window) | copy-start | bytes 9220
  75.0 18.6 %all-to-all-start.2 = ((bf16[256,2,128]{2,1,0:T(2,128)(2,1)}), bf16[256,2,128]{2,1,0:T(2,128)(2,1)S(1)}, u32[]{:S(2)}, u32[]{:S(2)}) async-start(bf16[256,2,128]{2,1,0:T(2,128)(2,1)} %bitcast.13), calls=%async_computation.2 | async-start | bytes 262144 | tf_op jit(solution)/shard_map/all_to_all | solution.py:408
  80.5 15.0 %collective-permute-start.9 = (bf16[512,128]{1,0:T(8,128)(2,1)S(1)}, bf16[512,128]{1,0:T(8,128)(2,1)S(1)}, u32[]{:S(2)}, u32[]{:S(2)}) collective-permute-start(bf16[512,128]{1,0:T(8,128)(2,1)S(1)} %get-tuple-element.16.refs_0_), channel_id=1, source_target_pairs={{0,1},{1,2},{2,3},{3,0},{4,5},{5,6},{6,7},{7,4},{8,9},{9,10},{10,1... | collective-permute-start | bytes 393224 | tf_op jit(solution)/shard_map/ppermute | solution.py:417
  82.2 14.3 %collective-permute-start.8 = (bf16[512,128]{1,0:T(8,128)(2,1)S(1)}, bf16[512,128]{1,0:T(8,128)(2,1)S(1)}, u32[]{:S(2)}, u32[]{:S(2)}) collective-permute-start(bf16[512,128]{1,0:T(8,128)(2,1)S(1)} %get-tuple-element.16.refs_0_), channel_id=1, source_target_pairs={{0,2},{1,3},{2,0},{3,1},{4,6},{5,7},{6,4},{7,5},{8,10},{9,11},{10,... | collective-permute-start | bytes 393224 | tf_op jit(solution)/shard_map/ppermute | solution.py:417
  84.8 13.0 %collective-permute-start.7 = (bf16[512,128]{1,0:T(8,128)(2,1)S(1)}, bf16[512,128]{1,0:T(8,128)(2,1)S(1)}, u32[]{:S(2)}, u32[]{:S(2)}) collective-permute-start(bf16[512,128]{1,0:T(8,128)(2,1)S(1)} %get-tuple-element.16.refs_0_), channel_id=1, source_target_pairs={{0,3},{1,0},{2,1},{3,2},{4,7},{5,4},{6,5},{7,6},{8,11},{9,8},{10,9... | collective-permute-start | bytes 393224 | tf_op jit(solution)/shard_map/ppermute | solution.py:417
  93.8 6.8 %collective-permute-start.6 = (bf16[512,128]{1,0:T(8,128)(2,1)S(1)}, bf16[512,128]{1,0:T(8,128)(2,1)S(1)}, u32[]{:S(2)}, u32[]{:S(2)}) collective-permute-start(bf16[512,128]{1,0:T(8,128)(2,1)S(1)} %fusion.own), channel_id=1, source_target_pairs={{0,192},{4,196},{1,0},{5,4},{2,1},{6,5},{3,2},{7,6},{32,3},{36,7},... | collective-permute-start | bytes 393224 | tf_op jit(solution)/shard_map/ppermute | solution.py:413
  94.7 6.0 %collective-permute-start.5 = (bf16[512,128]{1,0:T(8,128)(2,1)S(1)}, bf16[512,128]{1,0:T(8,128)(2,1)S(1)}, u32[]{:S(2)}, u32[]{:S(2)}) collective-permute-start(bf16[512,128]{1,0:T(8,128)(2,1)S(1)} %fusion.own), channel_id=1, source_target_pairs={{0,196},{4,0},{1,4},{5,1},{2,5},{6,2},{3,6},{7,3},{32,7},{36,32},{... | collective-permute-start | bytes 393224 | tf_op jit(solution)/shard_map/ppermute | solution.py:413
  95.4 5.3 %collective-permute-start.4 = (bf16[512,128]{1,0:T(8,128)(2,1)S(1)}, bf16[512,128]{1,0:T(8,128)(2,1)S(1)}, u32[]{:S(2)}, u32[]{:S(2)}) collective-permute-start(bf16[512,128]{1,0:T(8,128)(2,1)S(1)} %fusion.own), channel_id=1, source_target_pairs={{0,4},{4,1},{1,5},{5,2},{2,6},{6,3},{3,7},{7,32},{32,36},{36,33},{... | collective-permute-start | bytes 393224 | tf_op jit(solution)/shard_map/ppermute | solution.py:413
  96.5 7.0 %collective-permute-start.3 = (bf16[512,128]{1,0:T(8,128)(2,1)S(1)}, bf16[512,128]{1,0:T(8,128)(2,1)S(1)}, u32[]{:S(2)}, u32[]{:S(2)}) collective-permute-start(bf16[512,128]{1,0:T(8,128)(2,1)S(1)} %fusion.own), channel_id=1, source_target_pairs={{0,1},{4,5},{1,2},{5,6},{2,3},{6,7},{3,32},{7,36},{32,33},{36,37},... | collective-permute-start | bytes 393224 | tf_op jit(solution)/shard_map/ppermute | solution.py:413
  97.7 5.7 %copy-start.4 = (bf16[3,512,128]{2,1,0:T(8,128)(2,1)S(1)}, bf16[3,512,128]{2,1,0:T(8,128)(2,1)}, u32[]{:S(2)}) copy-start(bf16[3,512,128]{2,1,0:T(8,128)(2,1)} %constant.91.clone.window_back) | copy-start | bytes 1179652
  107.9 5.2 %collective-permute-start.13 = (bf16[512,128]{1,0:T(8,128)(2,1)S(1)}, bf16[512,128]{1,0:T(8,128)(2,1)S(1)}, u32[]{:S(2)}, u32[]{:S(2)}) collective-permute-start(bf16[512,128]{1,0:T(8,128)(2,1)S(1)} %get-tuple-element.17.own), channel_id=1, source_target_pairs={{0,192},{4,196},{1,0},{5,4},{2,1},{6,5},{3,2},{7,6},{32,3},{36,7},... | collective-permute-start | bytes 393224 | tf_op jit(solution)/shard_map/ppermute | solution.py:413
  108.2 6.7 %collective-permute-start.12 = (bf16[512,128]{1,0:T(8,128)(2,1)S(1)}, bf16[512,128]{1,0:T(8,128)(2,1)S(1)}, u32[]{:S(2)}, u32[]{:S(2)}) collective-permute-start(bf16[512,128]{1,0:T(8,128)(2,1)S(1)} %get-tuple-element.17.own), channel_id=1, source_target_pairs={{0,196},{4,0},{1,4},{5,1},{2,5},{6,2},{3,6},{7,3},{32,7},{36,32},{... | collective-permute-start | bytes 393224 | tf_op jit(solution)/shard_map/ppermute | solution.py:413
  109.0 5.9 %collective-permute-start.11 = (bf16[512,128]{1,0:T(8,128)(2,1)S(1)}, bf16[512,128]{1,0:T(8,128)(2,1)S(1)}, u32[]{:S(2)}, u32[]{:S(2)}) collective-permute-start(bf16[512,128]{1,0:T(8,128)(2,1)S(1)} %get-tuple-element.17.own), channel_id=1, source_target_pairs={{0,4},{4,1},{1,5},{5,2},{2,6},{6,3},{3,7},{7,32},{32,36},{36,33},{... | collective-permute-start | bytes 393224 | tf_op jit(solution)/shard_map/ppermute | solution.py:413
  109.9 6.8 %collective-permute-start.10 = (bf16[512,128]{1,0:T(8,128)(2,1)S(1)}, bf16[512,128]{1,0:T(8,128)(2,1)S(1)}, u32[]{:S(2)}, u32[]{:S(2)}) collective-permute-start(bf16[512,128]{1,0:T(8,128)(2,1)S(1)} %get-tuple-element.17.own), channel_id=1, source_target_pairs={{0,1},{4,5},{1,2},{5,6},{2,3},{6,7},{3,32},{7,36},{32,33},{36,37},... | collective-permute-start | bytes 393224 | tf_op jit(solution)/shard_map/ppermute | solution.py:413
  (2 other events, 2.2 us)
